TPU v7x, 256 devices: a whole 4x4x8 slice. The times are simulated.
256 devices in a mesh: query: 32 (over x, z), owner: 2 (over core), tensor: 4 (over y).
Axes of the slice: x: 4, y: 4, z: 8, core: 2. Of those that a mesh axis runs over, the one named last changes fastest.
Arguments:
- patches: bfloat16 [32, 2, 8, 257, 1408], P('query', 'owner'), may hold values from -64 to 64
- states: bfloat16 [2048, 32, 768], P(('query', 'owner')), may hold values from -64 to 64
- pair_source: int32 [2048, 1], P(('query', 'owner')), may hold values from 0 to 31; in each aligned block of 32 rows (0 to 31, 32 to 63, ...) at most 2 rows name the same one
- pair_image: int32 [2048], P(('query', 'owner')), may hold values from 0 to 7
- w_query: bfloat16 [768, 768], P(None, 'tensor'), may hold values from -0.21875 to 0.21875
- w_key: bfloat16 [1408, 768], P(None, 'tensor'), may hold values from -0.15625 to 0.15625
- w_value: bfloat16 [1408, 768], P(None, 'tensor'), may hold values from -0.15625 to 0.15625
- w_out: bfloat16 [768, 768], P('tensor'), may hold values from -0.21875 to 0.21875
- w_in: bfloat16 [768, 3072], P(None, 'tensor'), may hold values from -1 to 1
- w_down: bfloat16 [3072, 768], P('tensor'), may hold values from -2 to 2
- w_match: bfloat16 [768], replicated, may hold values from -1.25 to 1.25
Outputs:
- rankings: float32 [32, 64], P(None, 'owner')
Inputs may be any that keep to these rules, and one draw needn't show every extreme that they name: `pair_source`: among the pairs of one device no query index appears more than 2 times, and it appears exactly 2 times on some device.
All inputs are finite; a program needn't handle non-finite values.
Results may differ from a plain program's by a relative error of at most 0.0015.
Values may be sent and summed in bfloat16 or wider, within the bound.
A program may use at most 128 MiB of HBM per device.

v0:
```python
import jax
import jax.numpy as jnp
from jax import lax
from jax.sharding import PartitionSpec as P

HEAD_SIZE = 64


EPSILON = 1e-06


def attend_heads(queries, keys_values, head_size):
    batched, token_count, feature_width = queries.shape
    head_count = feature_width // head_size
    key_part = keys_values[:, :, :feature_width].reshape(batched, -1, head_count, head_size)
    value_part = keys_values[:, :, feature_width:].reshape(batched, -1, head_count, head_size)
    split_q = queries.reshape(batched, token_count, head_count, head_size)
    scores = jnp.einsum(
        "bqhd,bkhd->bhqk", split_q, key_part, preferred_element_type=jnp.float32
    ) * head_size ** (-0.5)
    highest = jnp.max(scores, axis=-1, keepdims=True)
    raised = jnp.exp(scores - highest)
    weights = (raised / jnp.sum(raised, axis=-1, keepdims=True)).astype(jnp.bfloat16)
    context = jnp.einsum("bhqk,bkhd->bqhd", weights, value_part, preferred_element_type=jnp.float32)
    return context.astype(jnp.bfloat16).reshape(batched, token_count, feature_width)


def normalize_whole(partial_value, residual):
    summed = lax.psum(partial_value, "tensor")
    blended = residual.astype(jnp.float32) + summed
    average = jnp.mean(blended, axis=-1, keepdims=True)
    squares = jnp.mean(blended * blended, axis=-1, keepdims=True)
    return (blended - average) * lax.rsqrt(squares - average * average + EPSILON)


def body(
    patches, states, pair_source, pair_image, w_query, w_key, w_value, w_out, w_in, w_down, w_match
):
    pair_count = states.shape[0]
    group_count = lax.axis_size("query")
    capacity = max(2, 2 * pair_count // group_count)
    slot_count = group_count * capacity
    source = pair_source[:, 0]
    chosen = (source[:, None] == jnp.arange(group_count, dtype=jnp.int32)[None, :]).astype(
        jnp.int32
    )
    before = jnp.cumsum(chosen, axis=0) - chosen
    position = jnp.sum(before * chosen, axis=1)
    slot_of = source * capacity + position
    placed = slot_of[None, :] == jnp.arange(slot_count, dtype=jnp.int32)[:, None]
    request = jnp.sum(jnp.where(placed, pair_image[None, :], 0), axis=1)
    image_count = patches.shape[2]
    key_value_weight = jnp.concatenate([w_key, w_value], axis=1)
    images_flat = patches.reshape(image_count, patches.shape[3], patches.shape[4])
    projected = jnp.dot(images_flat, key_value_weight, preferred_element_type=jnp.float32).astype(
        jnp.bfloat16
    )
    query_rows = jnp.dot(states, w_query, preferred_element_type=jnp.float32).astype(jnp.bfloat16)
    asked_for = lax.all_to_all(
        request.reshape(group_count, capacity), "query", split_axis=0, concat_axis=0, tiled=True
    )
    outgoing = projected[asked_for.reshape(-1)].reshape(
        group_count, capacity, projected.shape[1], projected.shape[2]
    )
    incoming = lax.all_to_all(outgoing, "query", split_axis=0, concat_axis=0, tiled=True)
    fetched = incoming.reshape(slot_count, projected.shape[1], projected.shape[2])[slot_of]
    context = attend_heads(query_rows, fetched, HEAD_SIZE)
    attended = jnp.dot(context, w_out, preferred_element_type=jnp.float32)
    match_dir = w_match.astype(jnp.float32)
    first_norm = normalize_whole(attended, states).astype(jnp.bfloat16)
    up_proj = jnp.dot(first_norm, w_in, preferred_element_type=jnp.float32)
    hidden = jax.nn.gelu(up_proj, approximate=False).astype(jnp.bfloat16)
    fed = jnp.dot(hidden, w_down, preferred_element_type=jnp.float32)
    second_norm = normalize_whole(fed, first_norm)
    match_score = jnp.mean(jnp.sum(second_norm * match_dir, axis=-1), axis=1)
    partition = lax.psum(jnp.sum(jnp.exp(match_score)), "owner")
    ranked = (match_score - jnp.log(partition))[None, :]
    return lax.all_gather(ranked, "query", axis=0, tiled=True)


def solution(mesh):
    placed = (
        P("query", "owner", None, None, None),
        P(("query", "owner"), None, None),
        P(("query", "owner"), None),
        P(("query", "owner")),
        P(None, "tensor"),
        P(None, "tensor"),
        P(None, "tensor"),
        P("tensor", None),
        P(None, "tensor"),
        P("tensor", None),
        P(),
    )
    return jax.shard_map(
        body, mesh=mesh, in_specs=placed, out_specs=P(None, "owner"), check_vma=False
    )
```

profile of v0, /device:TPU:1, one launch (start us, length us, event | category | flops | bytes accessed | tf_op | source)
XLA Modules:
  0.0 689.2 jit_solution(6557950272417920129)
XLA Ops:
  6.5 0.8 fusion.39
  7.4 0.8 select_reduce_fusion.1
  8.3 0.7 multiply_add_fusion
  8.9 0.7 select_reduce_fusion
  9.7 0.7 all_to_all.9
  10.4 11.9 %all-to-all-start = ((s32[32,1,2]{2,1,0:T(1,128)}), s32[32,1,2]{2,1,0:T(1,128)S(1)}, u32[]{:S(2)}, u32[]{:S(2)}) async-start(s32[32,1,2]{2,1,0:T(1,128)} %bitcast.4), calls=%async_computation | async-start | bytes 32768 | tf_op jit(solution)/shard_map/all_to_all | solution.py:59
  22.3 1.3 copy.33
  23.6 2.2 copy.34
  25.8 6.4 fusion.22
  32.2 0.5 broadcast.136
  32.7 0.7 reduce.8
  33.5 7.5 %gather_fusion = bf16[64,257,384]{2,1,0:T(8,128)(2,1)} fusion(bf16[8,257,384]{2,1,0:T(8,128)(2,1)S(1)} %fusion.22, s32[1024]{0:T(1024)S(1)} %pad_clamp_fusion.1), kind=kCustom, calls=%fused_computation | custom fusion | bytes 25264384 | tf_op jit(solution)/shard_map/gather | solution.py:62
  41.0 18.9 %copy.37 = bf16[32,2,257,384]{3,1,2,0:T(2,128)(2,1)} copy(bf16[32,2,257,384]{3,2,1,0:T(8,128)(2,1)} %bitcast.43) | data formatting | bytes 25264128 | tf_op jit(solution)/shard_map/reshape | solution.py:62
  59.8 9.5 %all-to-all-start.1 = ((bf16[32,2,257,384]{3,1,2,0:T(2,128)(2,1)}), bf16[32,2,257,384]{3,1,2,0:T(2,128)(2,1)}, u32[]{:S(2)}, u32[]{:S(2)}) async-start(bf16[32,2,257,384]{3,1,2,0:T(2,128)(2,1)} %copy.37), calls=%async_computation.1 | async-start | bytes 25264128 | tf_op jit(solution)/shard_map/all_to_all | solution.py:65
  69.4 0.2 all-reduce.4.cloned.1.call-start
  69.6 1.6 convolution_convert_fusion
  71.2 1.2 reshape.125
  72.3 281.2 %all-to-all-done.1 = bf16[32,2,257,384]{3,1,2,0:T(2,128)(2,1)} async-done(((bf16[32,2,257,384]{3,1,2,0:T(2,128)(2,1)}), bf16[32,2,257,384]{3,1,2,0:T(2,128)(2,1)}, u32[]{:S(2)}, u32[]{:S(2)}) %all-to-all-start.1) | async-done | bytes 12632096 | tf_op jit(solution)/shard_map/all_to_all | solution.py:65
  353.5 11.8 %copy.38 = bf16[32,2,257,384]{3,2,1,0:T(8,128)(2,1)} copy(bf16[32,2,257,384]{3,1,2,0:T(2,128)(2,1)} %all-to-all-done.1) | data formatting | bytes 25264128 | tf_op jit(solution)/shard_map/all_to_all | solution.py:65
  365.3 9.0 %gather_fusion.1 = bf16[32,257,384]{2,1,0:T(8,128)(2,1)} fusion(bf16[64,257,384]{2,1,0:T(8,128)(2,1)} %bitcast.44, s32[1024]{0:T(1024)S(1)} %pad_clamp_fusion), kind=kCustom, calls=%fused_computation.1 | custom fusion | bytes 12632192 | tf_op jit(solution)/shard_map/gather | solution.py:66
  374.3 6.8 fusion.75
  381.1 7.4 %copy.40 = bf16[32,257,192]{1,2,0:T(8,128)(2,1)} copy(bf16[32,257,192]{2,1,0:T(8,128)(2,1)} %get-tuple-element.11) | data formatting | bytes 6316032 | tf_op jit(solution)/shard_map/slice | solution.py:15
  388.5 3.6 fusion.34
  392.1 3.2 fusion.76
  395.3 7.4 %copy.39 = bf16[32,257,192]{1,2,0:T(8,128)(2,1)} copy(bf16[32,257,192]{2,1,0:T(8,128)(2,1)} %get-tuple-element.12) | data formatting | bytes 6316032 | tf_op jit(solution)/shard_map/slice | solution.py:16
  402.7 5.6 fusion.26
  408.3 1.5 copy.42
  409.8 2.5 reshape.127
  412.3 3.2 fusion.36
  415.5 0.3 all-reduce.6.cloned.1.call-start
  415.8 99.6 %all-reduce.4.cloned.1.call-done = f32[32,32,768]{2,1,0:T(8,128)} async-done(((f32[32,32,768]{2,1,0:T(8,128)}), f32[32,32,768]{2,1,0:T(8,128)}) %all-reduce.4.cloned.1.call-update) | async-done | bytes 3145744 | tf_op jit(solution)/shard_map/psum | solution.py:29
  515.4 2.7 fusion.27
  518.1 0.1 copy-done.2
  518.3 0.5 copy-done.4
  518.7 0.5 multiply_convert_fusion
  519.2 1.8 convert_reduce_fusion.1
  521.1 9.5 %fusion.20 = f32[32,32,768]{2,1,0:T(8,128)} fusion(f32[32,32,768]{2,1,0:T(8,128)S(1)} %get-tuple-element.19, u32[32,768]{1,0:T(8,128)S(1)} %get-tuple-element.10, u32[32,768]{1,0:T(8,128)S(1)} %get-tuple-element.9, bf16[768,768]{1,0:T(8,128)(2,1)S(1)} %copy-done.7), kind=kOutput, calls=%fused_computation.40 | convolution fusion | flops 1261436928 | bytes 7667712 | tf_op jit(solution)/shard_map/dot_general | solution.py:73
  530.6 0.6 copy-done.5
  531.2 0.6 dynamic-slice
  531.8 79.7 %all-reduce.6.cloned.1.call-done = f32[32,32,768]{2,1,0:T(8,128)} async-done(((f32[32,32,768]{2,1,0:T(8,128)}), f32[32,32,768]{2,1,0:T(8,128)}) %all-reduce.6.cloned.1.call-update) | async-done | bytes 3145744 | tf_op jit(solution)/shard_map/psum | solution.py:29
  611.5 2.7 fusion.28
  614.2 0.1 copy-done.1
  614.3 0.9 multiply_reduce_fusion.1
  615.2 0.7 exponential_reduce_fusion
  616.6 3.4 psum.23
  620.7 0.1 subtract_dynamic-update-slice_fusion
  620.8 60.9 %all-reduce = f32[1024]{0:T(1024)S(1)} all-reduce(f32[1024]{0:T(1024)S(1)} %subtract_dynamic-update-slice_fusion), channel_id=2, replica_groups=mesh['query'=32,'owner'=2,'tensor'=4] {'query'}, use_global_device_ids=true, to_apply=%add | all-reduce | flops 1024 | bytes 8192
  681.7 0.7 reshape.144
  (27 shorter events, 0.3 us)
Async XLA Ops:
  6.5 512.7 %copy-start = (bf16[768,768]{1,0:T(8,128)(2,1)S(1)}, bf16[768,768]{1,0:T(8,128)(2,1)}, u32[]{:S(2)}) copy-start(bf16[768,768]{1,0:T(8,128)(2,1)} %param.19) | copy-start | bytes 3538948
  10.4 21.8 %all-to-all-start = ((s32[32,1,2]{2,1,0:T(1,128)}), s32[32,1,2]{2,1,0:T(1,128)S(1)}, u32[]{:S(2)}, u32[]{:S(2)}) async-start(s32[32,1,2]{2,1,0:T(1,128)} %bitcast.4), calls=%async_computation | async-start | bytes 32768 | tf_op jit(solution)/shard_map/all_to_all | solution.py:59
  59.8 9.8 %copy-start.3 = (bf16[32,32,768]{2,1,0:T(8,128)(2,1)S(1)}, bf16[32,32,768]{2,1,0:T(8,128)(2,1)}, u32[]{:S(2)}) copy-start(bf16[32,32,768]{2,1,0:T(8,128)(2,1)} %param.12) | copy-start | bytes 4718596
  59.8 293.7 %all-to-all-start.1 = ((bf16[32,2,257,384]{3,1,2,0:T(2,128)(2,1)}), bf16[32,2,257,384]{3,1,2,0:T(2,128)(2,1)}, u32[]{:S(2)}, u32[]{:S(2)}) async-start(bf16[32,2,257,384]{3,1,2,0:T(2,128)(2,1)} %copy.37), calls=%async_computation.1 | async-start | bytes 25264128 | tf_op jit(solution)/shard_map/all_to_all | solution.py:65
  69.4 3.0 copy-start.6
  69.4 446.1 %all-reduce.4.cloned.1.call-start = ((), (), s32[]{:S(2)}) async-start(), calls=%async_computation.2 | async-start | bytes 6291456 | tf_op jit(solution)/shard_map/psum | solution.py:29
  415.5 195.9 %all-reduce.6.cloned.1.call-start = ((), (), s32[]{:S(2)}) async-start(), calls=%async_computation.3 | async-start | bytes 6291456 | tf_op jit(solution)/shard_map/psum | solution.py:29
  515.4 2.8 copy-start.2
  515.4 3.3 copy-start.4
  519.2 1.9 copy-start.7
  530.5 0.7 copy-start.5
  530.5 0.7 copy-start.8
  611.5 2.8 copy-start.1
Sparse Core Ops, SparseCore 0:
  415.7 99.7 all-reduce.3
  530.7 80.7 all-reduce.5
where the time goes:
time: 702 us; the launch traced here: 689 us
  waiting for transfers between devices  461 us (66%)
  local copies, waits for them, and re-layouts  81.3 us (12%)
  blocking collectives  64.3 us (9%)
  matrix products  31.6 us (5%)
  starting transfers between devices  21.8 us (3%)
  between operations  15 us (2%)
  other arithmetic  14.6 us (2%)
    all_to_all x1, waiting for transfers between devices, body(): lax.all_to_all(outgoing, 'query', split_axis=0, concat_axis=0, tiled=True)  281 us
    psum x2, waiting for transfers between devices, normalize_whole(): summed = lax.psum(partial_value, 'tensor')  179 us
    unnamed x1, blocking collectives  60.9 us
    reshape x1, local copies, waits for them, and re-layouts, body(): projected[asked_for.reshape(-1)]  18.9 us
    slice x2, local copies, waits for them, and re-layouts, attend_heads(): keys_values[:, :, :feature_width]  14.2 us
  transfers between devices with their start and end apart: 4, of which 3 were waited for; matrix products, arithmetic and copies ran while one was open for 2% of the time, Pallas kernels for 0%

commit v1 on v0

v1 whole, which is shorter than its diff:
```python
import functools

import jax
import jax.numpy as jnp
from jax import lax
from jax.experimental import pallas as pl
from jax.experimental.pallas import tpu as pltpu
from jax.sharding import PartitionSpec as P

D = 768
PATCH = 257
VIS = 1408
PAIRS = 32
NQ = 32
IMAGES = 8
SLOTS = 2
NX, NZ = 4, 8
GROUPS = NX * NZ
TENSOR = 4
PACK = 48
KEYS = 384
ROWS = PAIRS // TENSOR * NQ
EPSILON = 1e-06
MESH = pl.DeviceIdType.MESH
bf16, f32 = jnp.bfloat16, jnp.float32


def kernel(
    idx, img, states_h, patches_h, wq_h, wk_h, wv_h, wout_h, win_h, wdn_h, match_ref,
    out_ref,
    states, patches, wq, wk, wv, wqx, wkvx,
    qpk, qsend, qrecv, csend, crecv, keys, values, img_recv, img_s,
    ysend, yrecv, wout, win, wdn, fsend, frecv, ssend, srecv, osend, orecv,
    load_sem, img_ss, img_rs, q_ss, q_rs, c_ss, c_rs, y_ss, y_rs,
    w_own, w_ss, w_rs, f_ss, f_rs, s_ss, s_rs, o_ss, o_rs, img_sem,
):
    me = lax.axis_index("query")
    core = lax.axis_index("owner")
    ty = lax.axis_index("tensor")
    x, z = me // NZ, me % NZ

    def peer(k):
        iz, ix = k // NX, k % NX
        dz = ((iz + 1) // 2) * (2 * (iz % 2) - 1)
        dx = ((ix + 1) // 2) * (2 * (ix % 2) - 1)
        return ((x + dx + NX) % NX) * NZ + (z + dz + NZ) % NZ

    def y_peer(k):
        return (ty + k) % TENSOR

    def remote(src, dst, ss, rs, **device):
        return pltpu.make_async_remote_copy(
            src_ref=src, dst_ref=dst, send_sem=ss, recv_sem=rs, device_id=device, device_id_type=MESH
        )

    loads = [
        pltpu.make_async_copy(src, dst, load_sem.at[i])
        for i, (src, dst) in enumerate(
            ((states_h, states), (wq_h, wq), (wk_h, wk), (wv_h, wv), (patches_h.at[0, 0], patches))
        )
    ]
    for copy in loads:
        copy.start()

    barrier = pltpu.get_barrier_semaphore()

    @pl.loop(1, GROUPS)
    def _(k):
        pl.semaphore_signal(barrier, inc=1, device_id={"query": peer(k)}, device_id_type=MESH)

    for k in range(1, TENSOR):
        pl.semaphore_signal(barrier, inc=1, device_id={"tensor": y_peer(k)}, device_id_type=MESH)
    pl.semaphore_signal(barrier, inc=1, device_id={"owner": 1 - core}, device_id_type=MESH)

    loads[0].wait()
    loads[1].wait()
    w = wq[...]
    wqx[...] = jnp.concatenate([w, w[:, 128:]], axis=1)
    low = lax.broadcasted_iota(jnp.int32, (1, 128), 1) < 64

    @pl.loop(0, PAIRS // 4)
    def _(b):
        rows = states[pl.ds(b * 4, 4)].reshape(4 * NQ, D)
        q = jnp.dot(rows, wqx[...], preferred_element_type=f32).reshape(4, NQ, 256)
        first, second = q[:, :, :128], q[:, :, 128:]
        last = jnp.where(low[None], second[:, :16], second[:, 16:])
        qpk[pl.ds(b * 4, 4)] = jnp.concatenate([first, last], axis=1).astype(bf16)

    pl.semaphore_wait(barrier, GROUPS + TENSOR - 1)

    def img_copy(dst, src):
        return remote(img.at[dst], img_recv.at[src], img_ss.at[dst], img_rs.at[src], query=dst)

    @pl.loop(1, GROUPS)
    def _(k):
        img_copy(peer(k), me).start()

    def of(ref, p):
        return ref.at[pl.ds(p * SLOTS, SLOTS)]

    def q_copy(dst, src):
        return remote(of(qsend, dst), of(qrecv, src), q_ss.at[dst], q_rs.at[src], query=dst)

    def c_copy(dst, src):
        return remote(of(csend, dst), of(crecv, src), c_ss.at[dst], c_rs.at[src], query=dst)

    @pl.loop(0, GROUPS)
    def _(k):
        p = peer(k)
        for s in range(SLOTS):
            qsend[p * SLOTS + s] = qpk[idx[p * SLOTS + s]]

        @pl.when(k > 0)
        def _():
            q_copy(p, me).start()

    right, left, across = y_peer(1), y_peer(3), y_peer(2)
    shards = ((wout_h, wout, 192), (win_h, win, D), (wdn_h, wdn, D))

    def part(ref, t, size, begin, length):
        return ref.at[t, pl.ds(begin, length)]

    def own(i):
        src, dst, size = shards[i]
        return pltpu.make_async_copy(src, dst.at[ty, pl.ds(0, size)], w_own.at[i])

    def first_hop(i, to_right):
        src, dst, size = shards[i]
        begin = pl.multiple_of(core * (size // 2), size // 2)
        j = 0 if to_right else 1
        return remote(
            src.at[pl.ds(begin, size // 2)], dst.at[ty, pl.ds(begin, size // 2)],
            w_ss.at[i, j], w_rs.at[i, j], tensor=right if to_right else left,
        )

    def second_hop(i, to_right, receive=False):
        _, dst, size = shards[i]
        quarter = size // 4
        t = across if receive else (left if to_right else right)
        begin = pl.multiple_of(core * (size // 2) + (0 if to_right else quarter), quarter)
        place = dst.at[t, pl.ds(begin, quarter)]
        j = 2 if to_right else 3
        return remote(place, place, w_ss.at[i, j], w_rs.at[i, j], tensor=right if to_right else left)

    def sibling(i, which, receive=False):
        _, dst, size = shards[i]
        c = 1 - core if receive else core
        quarter = size // 4
        if which < 2:
            t, begin, length = (left if which == 0 else right), c * (size // 2), size // 2
        else:
            t, begin, length = across, c * (size // 2) + (which - 2) * quarter, quarter
        place = dst.at[t, pl.ds(pl.multiple_of(begin, quarter), length)]
        return remote(place, place, w_ss.at[i, 4 + which], w_rs.at[i, 4 + which], owner=1 - core)

    def weights_0(i):
        own(i).start()
        first_hop(i, True).start()
        first_hop(i, False).start()

    def weights_1(i):
        first_hop(i, True).wait_recv()
        second_hop(i, True).start()
        sibling(i, 0).start()
        first_hop(i, False).wait_recv()
        second_hop(i, False).start()
        sibling(i, 1).start()

    def weights_2(i):
        second_hop(i, True, True).wait_recv()
        sibling(i, 2).start()
        second_hop(i, False, True).wait_recv()
        sibling(i, 3).start()

    def weights_3(i):
        for which in range(4):
            sibling(i, which, True).wait_recv()
        own(i).wait()

    for i in range(3):
        weights_0(i)

    for copy in loads[2:]:
        copy.wait()
    w = wk[...]
    wkvx[:, :256] = jnp.concatenate([w, w[:, 128:]], axis=1)
    w = wv[...]
    wkvx[:, 256:] = jnp.concatenate([w, w[:, 128:]], axis=1)

    @pl.loop(0, IMAGES)
    def _(i):
        both = jnp.dot(patches[i], wkvx[...], preferred_element_type=f32).astype(bf16)
        pad = jnp.zeros((KEYS - 256, 256), bf16)
        keys[i, 256:KEYS] = pad
        values[i, 256:KEYS] = pad
        keys[i, 0:PATCH] = both[:, :256]
        values[i, 0:PATCH] = both[:, 256:]

    img_recv[me] = img[me]

    @pl.loop(1, GROUPS)
    def _(k):
        p = peer(k)
        img_copy(p, p).wait_recv()

    to_scalars = pltpu.make_async_copy(img_recv, img_s, img_sem)
    to_scalars.start()
    to_scalars.wait()

    first_mask = low.astype(f32).astype(bf16)
    second_mask = (1 - low.astype(f32)).astype(bf16)
    column = lax.broadcasted_iota(jnp.int32, (1, KEYS), 1)

    def attend(rows, image):
        a, b = rows[0:32], rows[32:48]
        top = jnp.concatenate([a * first_mask, a * second_mask, jnp.zeros((32, 128), bf16)], axis=0)
        bottom = jnp.concatenate([jnp.zeros((64, 128), bf16), b * first_mask, b * second_mask], axis=0)
        q = jnp.concatenate([top, bottom], axis=1)
        scores = lax.dot_general(q, keys[image], (((1,), (1,)), ((), ())), preferred_element_type=f32)
        scores = jnp.where(column < PATCH, scores * 0.125, -jnp.inf)
        raised = jnp.exp(scores - jnp.max(scores, axis=1, keepdims=True))
        weights = (raised / jnp.sum(raised, axis=1, keepdims=True)).astype(bf16)
        c = jnp.dot(weights, values[image], preferred_element_type=f32)
        c01 = jnp.where(low, c[0:32, :128], c[32:64, :128])
        c2 = jnp.where(low, c[64:80, 128:], c[80:96, 128:])
        return jnp.concatenate([c01, c2], axis=0).astype(bf16)

    qrecv[pl.ds(me * SLOTS, SLOTS)] = qsend[pl.ds(me * SLOTS, SLOTS)]

    @pl.loop(0, GROUPS)
    def _(k):
        p = peer(k)

        @pl.when(k > 0)
        def _():
            q_copy(p, p).wait_recv()

        done = [attend(qrecv[p * SLOTS + s], img_s[p, 0, s]) for s in range(SLOTS)]
        for s in range(SLOTS):
            csend[p * SLOTS + s] = done[s]

        @pl.when(k > 0)
        def _():
            c_copy(p, me).start()

    for i in range(3):
        weights_1(i)

    crecv[pl.ds(me * SLOTS, SLOTS)] = csend[pl.ds(me * SLOTS, SLOTS)]

    @pl.loop(1, GROUPS)
    def _(k):
        p = peer(k)
        c_copy(p, p).wait_recv()

    @pl.loop(0, PAIRS)
    def _(j):
        ysend[j // 8, j % 8] = crecv[idx[GROUPS * SLOTS + j]]

    def y_copy(dst, src):
        return remote(ysend.at[dst], yrecv.at[src], y_ss.at[dst], y_rs.at[src], tensor=dst)

    for k in range(1, TENSOR):
        y_copy(y_peer(k), ty).start()
    yrecv[ty] = ysend[ty]

    for i in range(3):
        weights_2(i)
    weights_3(0)
    for t in range(TENSOR):
        wout[t, 192:256] = wout[t, 128:192]
    for k in range(1, TENSOR):
        t = y_peer(k)
        y_copy(t, t).wait_recv()

    def norm(v):
        mean = jnp.mean(v, axis=-1, keepdims=True)
        squares = jnp.mean(v * v, axis=-1, keepdims=True)
        return (v - mean) * lax.rsqrt(squares - mean * mean + EPSILON)

    total = states[pl.ds(ty * 8, 8)].reshape(ROWS, D).astype(f32)
    for t in range(TENSOR):
        c = yrecv[t]
        b = c[:, 32:]
        second = jnp.concatenate([b * first_mask[None], b * second_mask[None]], axis=1)
        rows = jnp.concatenate([c[:, :32], second], axis=2).reshape(ROWS, 256)
        total = total + jnp.dot(rows, wout[t], preferred_element_type=f32)
    first_norm = norm(total).astype(bf16)

    for i in (1, 2):
        weights_3(i)
    total = first_norm.astype(f32)
    for t in range(TENSOR):
        for n in range(0, D, 256):
            up = jnp.dot(first_norm, win[t, :, n : n + 256], preferred_element_type=f32)
            hidden = (0.5 * up * (1.0 + lax.erf(up * 0.7071067811865476))).astype(bf16)
            total = total + jnp.dot(hidden, wdn[t, n : n + 256, :], preferred_element_type=f32)
    score = jnp.sum(norm(total) * match_ref[...].astype(f32), axis=-1, keepdims=True)
    score = jnp.mean(score.reshape(8, NQ, 1), axis=1)

    lane = lax.broadcasted_iota(jnp.int32, (8, 128), 1)
    pair = lax.broadcasted_iota(jnp.int32, (8, 128), 0) + (core * PAIRS + ty * 8)
    row = jnp.sum(jnp.where(lane == pair, score, 0.0), axis=0, keepdims=True)
    fsend[...] = row

    def f_copy(dst, src):
        return remote(fsend, frecv.at[src], f_ss.at[dst], f_rs.at[src], tensor=dst)

    for k in range(1, TENSOR):
        f_copy(y_peer(k), ty).start()
    frecv[ty] = row
    for k in range(1, TENSOR):
        t = y_peer(k)
        f_copy(t, t).wait_recv()
    row = frecv[0] + frecv[1] + frecv[2] + frecv[3]
    ssend[...] = row
    s_copy = remote(ssend, srecv, s_ss, s_rs, owner=1 - core)
    s_copy.start()
    s_copy.wait_recv()
    row = row + srecv[...]
    valid = lax.broadcasted_iota(jnp.int32, (1, 128), 1) < 2 * PAIRS
    partition = jnp.sum(jnp.where(valid, jnp.exp(row), 0.0), axis=1, keepdims=True)
    row = row - jnp.log(partition)
    row = jnp.where(core == 0, row, pltpu.roll(row, 128 - PAIRS, 1))
    osend[...] = row
    orecv[me] = row

    def o_copy(dst, src):
        return remote(osend, orecv.at[src], o_ss.at[dst], o_rs.at[src], query=dst)

    @pl.loop(1, GROUPS)
    def _(k):
        o_copy(peer(k), me).start()

    @pl.loop(1, GROUPS)
    def _(k):
        p = peer(k)
        o_copy(p, p).wait_recv()

    out_ref[...] = orecv[...].reshape(GROUPS, 128)[:, :PAIRS]

    @pl.loop(1, GROUPS)
    def _(k):
        p = peer(k)
        img_copy(p, p).wait_send()
        q_copy(p, p).wait_send()
        c_copy(p, p).wait_send()
        o_copy(p, p).wait_send()

    for k in range(1, TENSOR):
        t = y_peer(k)
        y_copy(t, t).wait_send()
        f_copy(t, t).wait_send()
    s_copy.wait_send()
    for i in range(3):
        first_hop(i, True).wait_send()
        first_hop(i, False).wait_send()
        second_hop(i, True).wait_send()
        second_hop(i, False).wait_send()
        for which in range(4):
            sibling(i, which).wait_send()


def body(
    patches, states, pair_source, pair_image, w_query, w_key, w_value, w_out, w_in, w_down, w_match
):
    source = pair_source[:, 0]
    number = jnp.arange(PAIRS, dtype=jnp.int32)
    earlier = (source[:, None] == source[None, :]) & (number[None, :] < number[:, None])
    slot_of = source * SLOTS + jnp.sum(earlier.astype(jnp.int32), axis=1)
    placed = slot_of[None, :] == jnp.arange(GROUPS * SLOTS, dtype=jnp.int32)[:, None]
    pair_of = jnp.sum(jnp.where(placed, number[None, :], 0), axis=1)
    idx = jnp.concatenate([pair_of, slot_of, jnp.zeros((32,), jnp.int32)])
    lanes = jnp.arange(128, dtype=jnp.int32)
    at = jnp.where(lanes < SLOTS, jnp.arange(GROUPS, dtype=jnp.int32)[:, None] * SLOTS + lanes, -1)
    img = jnp.sum(jnp.where(at[:, :, None] == slot_of, pair_image, 0), axis=2).reshape(GROUPS, 1, 128)

    vmem = pl.BlockSpec(memory_space=pltpu.VMEM)
    hbm = pl.BlockSpec(memory_space=pl.ANY)
    dma = pltpu.SemaphoreType.DMA
    return pl.pallas_call(
        kernel,
        out_shape=jax.ShapeDtypeStruct((GROUPS, PAIRS), f32),
        in_specs=[pl.BlockSpec(memory_space=pltpu.SMEM), vmem] + [hbm] * 8 + [vmem],
        out_specs=vmem,
        scratch_shapes=[
            pltpu.VMEM((PAIRS, NQ, D), bf16),
            pltpu.VMEM((IMAGES, PATCH, VIS), bf16),
            pltpu.VMEM((D, 192), bf16),
            pltpu.VMEM((VIS, 192), bf16),
            pltpu.VMEM((VIS, 192), bf16),
            pltpu.VMEM((D, 256), bf16),
            pltpu.VMEM((VIS, 512), bf16),
            pltpu.VMEM((PAIRS, PACK, 128), bf16),
            pltpu.VMEM((GROUPS * SLOTS, PACK, 128), bf16),
            pltpu.VMEM((GROUPS * SLOTS, PACK, 128), bf16),
            pltpu.VMEM((GROUPS * SLOTS, PACK, 128), bf16),
            pltpu.VMEM((GROUPS * SLOTS, PACK, 128), bf16),
            pltpu.VMEM((IMAGES, KEYS, 256), bf16),
            pltpu.VMEM((IMAGES, KEYS, 256), bf16),
            pltpu.VMEM((GROUPS, 1, 128), jnp.int32),
            pltpu.SMEM((GROUPS, 1, 128), jnp.int32),
            pltpu.VMEM((TENSOR, 8, PACK, 128), bf16),
            pltpu.VMEM((TENSOR, 8, PACK, 128), bf16),
            pltpu.VMEM((TENSOR, 256, D), bf16),
            pltpu.VMEM((TENSOR, D, D), bf16),
            pltpu.VMEM((TENSOR, D, D), bf16),
            pltpu.VMEM((1, 128), f32),
            pltpu.VMEM((TENSOR, 1, 128), f32),
            pltpu.VMEM((1, 128), f32),
            pltpu.VMEM((1, 128), f32),
            pltpu.VMEM((1, 128), f32),
            pltpu.VMEM((GROUPS, 1, 128), f32),
            dma((5,)),
            dma((GROUPS,)), dma((GROUPS,)),
            dma((GROUPS,)), dma((GROUPS,)),
            dma((GROUPS,)), dma((GROUPS,)),
            dma((TENSOR,)), dma((TENSOR,)),
            dma((3,)), dma((3, 8)), dma((3, 8)),
            dma((TENSOR,)), dma((TENSOR,)),
            dma, dma,
            dma((GROUPS,)), dma((GROUPS,)),
            dma,
        ],
        compiler_params=pltpu.CompilerParams(
            collective_id=0, has_side_effects=True, vmem_limit_bytes=56 * 1024 * 1024
        ),
    )(idx, img, states, patches, w_query, w_key, w_value, w_out, w_in, w_down, w_match.reshape(1, D))


def solution(mesh):
    placed = (
        P("query", "owner", None, None, None),
        P(("query", "owner"), None, None),
        P(("query", "owner"), None),
        P(("query", "owner")),
        P(None, "tensor"),
        P(None, "tensor"),
        P(None, "tensor"),
        P("tensor", None),
        P(None, "tensor"),
        P("tensor", None),
        P(),
    )
    return jax.shard_map(
        body, mesh=mesh, in_specs=placed, out_specs=P(None, "owner"), check_vma=False
    )
```

time: 702 us -> 112 us (0.16); the launches traced: 689 us -> 111 us
  waiting for transfers between devices: 461 us -> 0 us
  Pallas kernels: 0 us -> 94 us
  local copies, waits for them, and re-layouts: 81.3 us -> 13.7 us
  blocking collectives: 64.3 us -> 0 us
  matrix products: 31.6 us -> 0 us
  starting transfers between devices: 21.8 us -> 0 us
  between operations: 15 us -> 0.02 us
  other arithmetic: 14.6 us -> 3.75 us
    all_to_all x2 -> x0, waiting for transfers between devices: 281 us -> none  [the longest x1 281 us: body(): lax.all_to_all(outgoing, 'query', split_axis=0, concat_axis=0, tiled=True)]
    psum x2 -> x0, waiting for transfers between devices: 179 us -> none  [normalize_whole(): summed = lax.psum(partial_value, 'tensor')]
    pallas_call x0 -> x1, Pallas kernels: none -> 94 us  [body(): pl.pallas_call(kernel, out_shape=jax.ShapeDtypeStruct((GROUPS, PAIRS), f3...]
    unnamed x1 -> x0, blocking collectives: 60.9 us -> none
    dot_general x7 -> x0, matrix products: 31.6 us -> none  [the longest x1 9.46 us: body(): fed = jnp.dot(hidden, w_down, preferred_element_type=jnp.float32)]
    slice x3 -> x0, local copies, waits for them, and re-layouts: 21.6 us -> none  [the longest x2 14.2 us: attend_heads(): keys_values[:, :, :feature_width]]
    all_to_all x2 -> x0, starting transfers between devices: 21.4 us -> none  [the longest x1 11.9 us: body(): lax.all_to_all(request.reshape(group_count, capacity), 'query', split_axi...]
    reshape x4 -> x1, local copies, waits for them, and re-layouts: 22.6 us -> 1.27 us  [body(): w_match.reshape(1, D)]
  transfers between devices with their start and end apart: 4 -> 0, of which waited for: 3 -> 0; matrix products, arithmetic and copies ran while one was open for 2% -> 0% of each run, Pallas kernels for 0% -> 0%
where the time goes in v1:
time: 112 us; the launch traced here: 111 us
  Pallas kernels  94 us (84%)
  local copies, waits for them, and re-layouts  13.7 us (12%)
  other arithmetic  3.75 us (3%)
    pallas_call x1, Pallas kernels, body(): pl.pallas_call(kernel, out_shape=jax.ShapeDtypeStruct((GROUPS, PAIRS), f3...  94 us
    unnamed x7, local copies, waits for them, and re-layouts  12.5 us

profile of v1, /device:TPU:1, one launch (start us, length us, event | category | flops | bytes accessed | tf_op | source)
XLA Modules:
  0.0 111.5 jit_solution(7955018203482690143)
XLA Ops:
  0.0 0.0 copy-start
  0.0 0.9 convert_reduce_fusion
  0.9 0.7 multiply_add_fusion
  1.6 0.1 select_reduce_fusion.1
  1.7 0.6 pad_add_fusion.idx
  2.3 1.3 %reshape.59.match_ref = bf16[1,768]{1,0:T(2,128)(2,1)} reshape(bf16[768]{0:T(1024)(128)(2,1)} %param.21) | data formatting | bytes 3072 | tf_op jit(solution)/shard_map/reshape | solution.py:428
  3.5 0.1 add_select_fusion
  3.6 1.4 %select_reduce_fusion = s32[32,128]{1,0:T(8,128)} fusion(s32[32]{0:T(128)} %param.14, s32[32,128]{1,0:T(8,128)S(1)} %add_select_fusion, s32[32]{0:T(128)S(1)} %multiply_add_fusion), kind=kLoop, calls=%fused_computation | loop fusion | flops 389120 | bytes 33024 | tf_op jit(solution)/shard_map/reduce_sum | solution.py:376
  5.0 1.9 %copy.17.wq_h = bf16[768,192]{1,0:T(8,128)(2,1)} copy(bf16[768,192]{0,1:T(8,128)(2,1)} %param.15) | data formatting | bytes 589824 | tf_op args[4]
  6.9 2.2 %copy.18.wk_h = bf16[1408,192]{1,0:T(8,128)(2,1)} copy(bf16[1408,192]{0,1:T(8,128)(2,1)} %param.16) | data formatting | bytes 1081344 | tf_op args[5]
  9.1 0.0 copy-done
  9.1 1.2 %copy.19.wv_h = bf16[1408,192]{1,0:T(8,128)(2,1)} copy(bf16[1408,192]{0,1:T(8,128)(2,1)S(1)} %copy-done) | data formatting | bytes 1081344 | tf_op args[6]
  10.3 5.9 %copy.16.patches_h = bf16[1,1,8,257,1408]{4,3,2,1,0:T(8,128)(2,1)} copy(bf16[1,1,8,257,1408]{4,2,3,1,0:T(8,128)(2,1)} %param.11) | data formatting | bytes 11579392 | tf_op args[0]
  16.2 94.0 %shard_map.109 = f32[32,32]{1,0:T(8,128)} custom-call(s32[128]{0:T(128)} %pad_add_fusion.idx, s32[32,1,128]{2,1,0:T(1,128)} %bitcast.3, bf16[32,32,768]{2,1,0:T(8,128)(2,1)} %states_h.1, bf16[1,1,8,257,1408]{4,3,2,1,0:T(8,128)(2,1)} %copy.16.patches_h, bf16[768,192]{1,0:T(8,128)(2,1)} %copy.17.wq_h, bf16[1408,192]{1,0:T(8,128)(2,1)} %copy.18.wk_h, ...), custom_call_target="tpu_custom_call" | custom-call | tf_op jit(solution)/shard_map/pallas_call | solution.py:381
  110.2 1.3 %copy.21 = f32[32,32]{1,0:T(8,128)} copy(f32[32,32]{1,0:T(8,128)} %shard_map.109) | data formatting | bytes 8192
  (3 shorter events, 0.0 us)
Async XLA Ops:
  0.0 9.1 %copy-start = (bf16[1408,192]{0,1:T(8,128)(2,1)S(1)}, bf16[1408,192]{0,1:T(8,128)(2,1)}, u32[]{:S(2)}) copy-start(bf16[1408,192]{0,1:T(8,128)(2,1)} %param.17) | copy-start | bytes 1622020

commit v2 on v1

--- a/solution.py
+++ b/solution.py
@@ -26,13 +26,13 @@
 
 
 def kernel(
-    idx, img, states_h, patches_h, wq_h, wk_h, wv_h, wout_h, win_h, wdn_h, match_ref,
+    source, image, match_ref, states_h, patches_h, wq_h, wk_h, wv_h, wout_h, win_h, wdn_h,
     out_ref,
-    states, patches, wq, wk, wv, wqx, wkvx,
+    states, patches, wqx, wkvx, both, img, idx_v, idx,
     qpk, qsend, qrecv, csend, crecv, keys, values, img_recv, img_s,
     ysend, yrecv, wout, win, wdn, fsend, frecv, ssend, srecv, osend, orecv,
     load_sem, img_ss, img_rs, q_ss, q_rs, c_ss, c_rs, y_ss, y_rs,
-    w_own, w_ss, w_rs, f_ss, f_rs, s_ss, s_rs, o_ss, o_rs, img_sem,
+    w_own, w_ss, w_rs, f_ss, f_rs, s_ss, s_rs, o_ss, o_rs, img_sem, idx_sem,
 ):
     me = lax.axis_index("query")
     core = lax.axis_index("owner")
@@ -56,7 +56,13 @@
     loads = [
         pltpu.make_async_copy(src, dst, load_sem.at[i])
         for i, (src, dst) in enumerate(
-            ((states_h, states), (wq_h, wq), (wk_h, wk), (wv_h, wv), (patches_h.at[0, 0], patches))
+            (
+                (states_h, states),
+                (wq_h, wqx.at[pl.ds(0, 192)]),
+                (wk_h, wkvx.at[pl.ds(0, 192)]),
+                (wv_h, wkvx.at[pl.ds(256, 192)]),
+                (patches_h, patches),
+            )
         )
     ]
     for copy in loads:
@@ -72,24 +78,48 @@
         pl.semaphore_signal(barrier, inc=1, device_id={"tensor": y_peer(k)}, device_id_type=MESH)
     pl.semaphore_signal(barrier, inc=1, device_id={"owner": 1 - core}, device_id_type=MESH)
 
+    wide = (PAIRS, 128)
+    lanes = lax.broadcasted_iota(jnp.int32, wide, 1)
+    number = lax.broadcasted_iota(jnp.int32, wide, 0)
+
+    def row_of(v):
+        return jnp.sum(v, axis=0, keepdims=True)
+
+    def column_of(v):
+        return jnp.sum(jnp.where(lanes == number, v, 0), axis=1, keepdims=True)
+
+    source_row = jnp.concatenate([source[...], jnp.full((1, 128 - PAIRS), -1, jnp.int32)], axis=1)
+    image_row = jnp.concatenate([image[...], jnp.zeros((1, 128 - PAIRS), jnp.int32)], axis=1)
+    earlier = (column_of(source_row) == source_row) & (number < lanes)
+    slot_row = source_row * SLOTS + row_of(earlier.astype(jnp.int32))
+    placed = column_of(slot_row) == lanes
+    img[...] = row_of(jnp.where(placed, column_of(image_row), 0))
+    idx_v[0:1] = row_of(jnp.where(placed, number, 0))
+    idx_v[1:2] = slot_row
+    to_index = pltpu.make_async_copy(idx_v, idx, idx_sem)
+    to_index.start()
+
     loads[0].wait()
     loads[1].wait()
-    w = wq[...]
-    wqx[...] = jnp.concatenate([w, w[:, 128:]], axis=1)
+    wqx[192:256] = wqx[128:192]
     low = lax.broadcasted_iota(jnp.int32, (1, 128), 1) < 64
+
+    def times(a, b):
+        return lax.dot_general(a, b, (((1,), (1,)), ((), ())), preferred_element_type=f32)
 
     @pl.loop(0, PAIRS // 4)
     def _(b):
         rows = states[pl.ds(b * 4, 4)].reshape(4 * NQ, D)
-        q = jnp.dot(rows, wqx[...], preferred_element_type=f32).reshape(4, NQ, 256)
+        q = times(rows, wqx[...]).reshape(4, NQ, 256)
         first, second = q[:, :, :128], q[:, :, 128:]
         last = jnp.where(low[None], second[:, :16], second[:, 16:])
         qpk[pl.ds(b * 4, 4)] = jnp.concatenate([first, last], axis=1).astype(bf16)
 
     pl.semaphore_wait(barrier, GROUPS + TENSOR - 1)
+    to_index.wait()
 
     def img_copy(dst, src):
-        return remote(img.at[dst], img_recv.at[src], img_ss.at[dst], img_rs.at[src], query=dst)
+        return remote(img, img_recv.at[src], img_ss.at[dst], img_rs.at[src], query=dst)
 
     @pl.loop(1, GROUPS)
     def _(k):
@@ -108,7 +138,7 @@
     def _(k):
         p = peer(k)
         for s in range(SLOTS):
-            qsend[p * SLOTS + s] = qpk[idx[p * SLOTS + s]]
+            qsend[p * SLOTS + s] = qpk[idx[0, p * SLOTS + s]]
 
         @pl.when(k > 0)
         def _():
@@ -182,21 +212,31 @@
 
     for copy in loads[2:]:
         copy.wait()
-    w = wk[...]
-    wkvx[:, :256] = jnp.concatenate([w, w[:, 128:]], axis=1)
-    w = wv[...]
-    wkvx[:, 256:] = jnp.concatenate([w, w[:, 128:]], axis=1)
+    wkvx[192:256] = wkvx[128:192]
+    wkvx[448:512] = wkvx[384:448]
+
+    @pl.loop(0, 8)
+    def _(i):
+        rows = patches[pl.ds(i * 32, 32)].reshape(256, VIS)
+        result = times(rows, wkvx[...])
+        for c in range(4):
+            both[c, pl.ds(i * 256, 256)] = result[:, c * 128 : c * 128 + 128]
+
+    result = times(patches[256], wkvx[...])
+    for c in range(4):
+        both[c, 2048:2056] = result[:, c * 128 : c * 128 + 128]
 
     @pl.loop(0, IMAGES)
     def _(i):
-        both = jnp.dot(patches[i], wkvx[...], preferred_element_type=f32).astype(bf16)
         pad = jnp.zeros((KEYS - 256, 256), bf16)
         keys[i, 256:KEYS] = pad
         values[i, 256:KEYS] = pad
-        keys[i, 0:PATCH] = both[:, :256]
-        values[i, 0:PATCH] = both[:, 256:]
-
-    img_recv[me] = img[me]
+        for c in range(4):
+            ref = keys if c < 2 else values
+            part = both[c, pl.ds(i, PATCH, stride=IMAGES)].astype(bf16)
+            ref[i, 0:PATCH, (c % 2) * 128 : (c % 2) * 128 + 128] = part
+
+    img_recv[me] = img[...]
 
     @pl.loop(1, GROUPS)
     def _(k):
@@ -216,7 +256,7 @@
         top = jnp.concatenate([a * first_mask, a * second_mask, jnp.zeros((32, 128), bf16)], axis=0)
         bottom = jnp.concatenate([jnp.zeros((64, 128), bf16), b * first_mask, b * second_mask], axis=0)
         q = jnp.concatenate([top, bottom], axis=1)
-        scores = lax.dot_general(q, keys[image], (((1,), (1,)), ((), ())), preferred_element_type=f32)
+        scores = times(q, keys[image])
         scores = jnp.where(column < PATCH, scores * 0.125, -jnp.inf)
         raised = jnp.exp(scores - jnp.max(scores, axis=1, keepdims=True))
         weights = (raised / jnp.sum(raised, axis=1, keepdims=True)).astype(bf16)
@@ -235,7 +275,7 @@
         def _():
             q_copy(p, p).wait_recv()
 
-        done = [attend(qrecv[p * SLOTS + s], img_s[p, 0, s]) for s in range(SLOTS)]
+        done = [attend(qrecv[p * SLOTS + s], img_s[p, 0, me * SLOTS + s]) for s in range(SLOTS)]
         for s in range(SLOTS):
             csend[p * SLOTS + s] = done[s]
 
@@ -255,7 +295,7 @@
 
     @pl.loop(0, PAIRS)
     def _(j):
-        ysend[j // 8, j % 8] = crecv[idx[GROUPS * SLOTS + j]]
+        ysend[j // 8, j % 8] = crecv[idx[1, j]]
 
     def y_copy(dst, src):
         return remote(ysend.at[dst], yrecv.at[src], y_ss.at[dst], y_rs.at[src], tensor=dst)
@@ -295,7 +335,7 @@
             up = jnp.dot(first_norm, win[t, :, n : n + 256], preferred_element_type=f32)
             hidden = (0.5 * up * (1.0 + lax.erf(up * 0.7071067811865476))).astype(bf16)
             total = total + jnp.dot(hidden, wdn[t, n : n + 256, :], preferred_element_type=f32)
-    score = jnp.sum(norm(total) * match_ref[...].astype(f32), axis=-1, keepdims=True)
+    score = jnp.sum(norm(total) * match_ref[...].astype(f32).reshape(1, D), axis=-1, keepdims=True)
     score = jnp.mean(score.reshape(8, NQ, 1), axis=1)
 
     lane = lax.broadcasted_iota(jnp.int32, (8, 128), 1)
@@ -364,33 +404,23 @@
 def body(
     patches, states, pair_source, pair_image, w_query, w_key, w_value, w_out, w_in, w_down, w_match
 ):
-    source = pair_source[:, 0]
-    number = jnp.arange(PAIRS, dtype=jnp.int32)
-    earlier = (source[:, None] == source[None, :]) & (number[None, :] < number[:, None])
-    slot_of = source * SLOTS + jnp.sum(earlier.astype(jnp.int32), axis=1)
-    placed = slot_of[None, :] == jnp.arange(GROUPS * SLOTS, dtype=jnp.int32)[:, None]
-    pair_of = jnp.sum(jnp.where(placed, number[None, :], 0), axis=1)
-    idx = jnp.concatenate([pair_of, slot_of, jnp.zeros((32,), jnp.int32)])
-    lanes = jnp.arange(128, dtype=jnp.int32)
-    at = jnp.where(lanes < SLOTS, jnp.arange(GROUPS, dtype=jnp.int32)[:, None] * SLOTS + lanes, -1)
-    img = jnp.sum(jnp.where(at[:, :, None] == slot_of, pair_image, 0), axis=2).reshape(GROUPS, 1, 128)
-
     vmem = pl.BlockSpec(memory_space=pltpu.VMEM)
     hbm = pl.BlockSpec(memory_space=pl.ANY)
     dma = pltpu.SemaphoreType.DMA
     return pl.pallas_call(
         kernel,
         out_shape=jax.ShapeDtypeStruct((GROUPS, PAIRS), f32),
-        in_specs=[pl.BlockSpec(memory_space=pltpu.SMEM), vmem] + [hbm] * 8 + [vmem],
+        in_specs=[vmem] * 3 + [hbm] * 8,
         out_specs=vmem,
         scratch_shapes=[
             pltpu.VMEM((PAIRS, NQ, D), bf16),
-            pltpu.VMEM((IMAGES, PATCH, VIS), bf16),
-            pltpu.VMEM((D, 192), bf16),
-            pltpu.VMEM((VIS, 192), bf16),
-            pltpu.VMEM((VIS, 192), bf16),
-            pltpu.VMEM((D, 256), bf16),
-            pltpu.VMEM((VIS, 512), bf16),
+            pltpu.VMEM((PATCH, IMAGES, VIS), bf16),
+            pltpu.VMEM((256, D), bf16),
+            pltpu.VMEM((512, VIS), bf16),
+            pltpu.VMEM((4, PATCH * IMAGES, 128), f32),
+            pltpu.VMEM((1, 128), jnp.int32),
+            pltpu.VMEM((2, 128), jnp.int32),
+            pltpu.SMEM((2, 128), jnp.int32),
             pltpu.VMEM((PAIRS, PACK, 128), bf16),
             pltpu.VMEM((GROUPS * SLOTS, PACK, 128), bf16),
             pltpu.VMEM((GROUPS * SLOTS, PACK, 128), bf16),
@@ -420,12 +450,15 @@
             dma((TENSOR,)), dma((TENSOR,)),
             dma, dma,
             dma((GROUPS,)), dma((GROUPS,)),
-            dma,
+            dma, dma,
         ],
         compiler_params=pltpu.CompilerParams(
             collective_id=0, has_side_effects=True, vmem_limit_bytes=56 * 1024 * 1024
         ),
-    )(idx, img, states, patches, w_query, w_key, w_value, w_out, w_in, w_down, w_match.reshape(1, D))
+    )(
+        pair_source.reshape(1, PAIRS), pair_image.reshape(1, PAIRS), w_match, states,
+        jnp.transpose(patches[0, 0], (1, 0, 2)), w_query.T, w_key.T, w_value.T, w_out, w_in, w_down,
+    )
 
 
 def solution(mesh):

time: 112 us -> 97.4 us (0.87)
  local copies, waits for them, and re-layouts: 13.7 us -> 1.32 us
  other arithmetic: 3.75 us -> 0 us
  Pallas kernels: 94 us -> 95.9 us
    unnamed x7 -> x1, local copies, waits for them, and re-layouts: 12.5 us -> 1.32 us
    reduce_sum x3 -> x0, other arithmetic: 2.41 us -> none  [the longest x1 1.41 us: body(): jnp.sum(jnp.where(at[:, :, None] == slot_of, pair_image, 0), axis=2)]
    pallas_call x1, Pallas kernels: 94 us -> 95.9 us  [body(): pl.pallas_call(kernel, out_shape=jax.ShapeDtypeStruct((GROUPS, PAIRS), f3...]
    reshape x1 -> x0, local copies, waits for them, and re-layouts: 1.27 us -> none  [body(): w_match.reshape(1, D)]
where the time goes in v2:
time: 97.4 us; the launch traced here: 97.3 us
  Pallas kernels  95.9 us (98%)
  local copies, waits for them, and re-layouts  1.32 us (1%)
    pallas_call x1, Pallas kernels, body(): pl.pallas_call(kernel, out_shape=jax.ShapeDtypeStruct((GROUPS, PAIRS), f3...  95.9 us

profile of v2, /device:TPU:1, one launch (start us, length us, event | category | flops | bytes accessed | tf_op | source)
XLA Modules:
  0.0 97.3 jit_solution(17886498725655770178)
XLA Ops:
  0.0 95.9 %shard_map.109 = f32[32,32]{1,0:T(8,128)} custom-call(s32[1,32]{1,0:T(1,128)} %bitcast.12, s32[1,32]{1,0:T(1,128)} %bitcast.13, bf16[768]{0:T(1024)(128)(2,1)} %match_ref.1, bf16[32,32,768]{2,1,0:T(8,128)(2,1)} %states_h.1, bf16[257,8,1408]{2,1,0:T(8,128)(2,1)} %bitcast.8, bf16[192,768]{1,0:T(8,128)(2,1)} %bitcast.11, bf16[192,1408]{1,0:T(8,128)(2,1)} %bitcast.9, ...), custom_call_target="tpu_custom_call" | custom-call | tf_op jit(solution)/shard_map/pallas_call | solution.py:410
  95.9 1.3 %copy.13 = f32[32,32]{1,0:T(8,128)} copy(f32[32,32]{1,0:T(8,128)} %shard_map.109) | data formatting | bytes 8192

commit v3 on v2

--- a/solution.py
+++ b/solution.py
@@ -37,16 +37,22 @@
     me = lax.axis_index("query")
     core = lax.axis_index("owner")
     ty = lax.axis_index("tensor")
-    x, z = me // NZ, me % NZ
+    x, z = lax.div(me, NZ), lax.rem(me, NZ)
+
+    def step(i):
+        return lax.div(i + 1, 2) * (2 * lax.rem(i, 2) - 1)
 
     def peer(k):
-        iz, ix = k // NX, k % NX
-        dz = ((iz + 1) // 2) * (2 * (iz % 2) - 1)
-        dx = ((ix + 1) // 2) * (2 * (ix % 2) - 1)
-        return ((x + dx + NX) % NX) * NZ + (z + dz + NZ) % NZ
+        return lax.rem(x + step(lax.rem(k, NX)) + NX, NX) * NZ + lax.rem(z + step(lax.div(k, NX)) + NZ, NZ)
+
+    steps = [((i + 1) // 2) * (2 * (i % 2) - 1) for i in range(NZ)]
+    columns = [lax.rem(x + steps[i] + NX, NX) * NZ for i in range(NX)]
+    rows_z = [lax.rem(z + steps[i] + NZ, NZ) for i in range(NZ)]
+    peers = [columns[k % NX] + rows_z[k // NX] for k in range(GROUPS)]
+    others = peers[1:]
 
     def y_peer(k):
-        return (ty + k) % TENSOR
+        return lax.rem(ty + k, TENSOR)
 
     def remote(src, dst, ss, rs, **device):
         return pltpu.make_async_remote_copy(
@@ -70,9 +76,8 @@
 
     barrier = pltpu.get_barrier_semaphore()
 
-    @pl.loop(1, GROUPS)
-    def _(k):
-        pl.semaphore_signal(barrier, inc=1, device_id={"query": peer(k)}, device_id_type=MESH)
+    for p in reversed(others):
+        pl.semaphore_signal(barrier, inc=1, device_id={"query": p}, device_id_type=MESH)
 
     for k in range(1, TENSOR):
         pl.semaphore_signal(barrier, inc=1, device_id={"tensor": y_peer(k)}, device_id_type=MESH)
@@ -107,13 +112,9 @@
     def times(a, b):
         return lax.dot_general(a, b, (((1,), (1,)), ((), ())), preferred_element_type=f32)
 
-    @pl.loop(0, PAIRS // 4)
-    def _(b):
-        rows = states[pl.ds(b * 4, 4)].reshape(4 * NQ, D)
-        q = times(rows, wqx[...]).reshape(4, NQ, 256)
-        first, second = q[:, :, :128], q[:, :, 128:]
-        last = jnp.where(low[None], second[:, :16], second[:, 16:])
-        qpk[pl.ds(b * 4, 4)] = jnp.concatenate([first, last], axis=1).astype(bf16)
+    q = times(states[...].reshape(PAIRS * NQ, D), wqx[...]).reshape(PAIRS, NQ, 256)
+    last = jnp.where(low[None], q[:, :16, 128:], q[:, 16:, 128:])
+    qpk[...] = jnp.concatenate([q[:, :, :128], last], axis=1).astype(bf16)
 
     pl.semaphore_wait(barrier, GROUPS + TENSOR - 1)
     to_index.wait()
@@ -121,9 +122,8 @@
     def img_copy(dst, src):
         return remote(img, img_recv.at[src], img_ss.at[dst], img_rs.at[src], query=dst)
 
-    @pl.loop(1, GROUPS)
-    def _(k):
-        img_copy(peer(k), me).start()
+    for p in others:
+        img_copy(p, me).start()
 
     def of(ref, p):
         return ref.at[pl.ds(p * SLOTS, SLOTS)]
@@ -134,14 +134,10 @@
     def c_copy(dst, src):
         return remote(of(csend, dst), of(crecv, src), c_ss.at[dst], c_rs.at[src], query=dst)
 
-    @pl.loop(0, GROUPS)
-    def _(k):
-        p = peer(k)
+    for k, p in enumerate(peers):
         for s in range(SLOTS):
             qsend[p * SLOTS + s] = qpk[idx[0, p * SLOTS + s]]
-
-        @pl.when(k > 0)
-        def _():
+        if k:
             q_copy(p, me).start()
 
     right, left, across = y_peer(1), y_peer(3), y_peer(2)
@@ -215,12 +211,12 @@
     wkvx[192:256] = wkvx[128:192]
     wkvx[448:512] = wkvx[384:448]
 
-    @pl.loop(0, 8)
+    @pl.loop(0, 4)
     def _(i):
-        rows = patches[pl.ds(i * 32, 32)].reshape(256, VIS)
+        rows = patches[pl.ds(i * 64, 64)].reshape(512, VIS)
         result = times(rows, wkvx[...])
         for c in range(4):
-            both[c, pl.ds(i * 256, 256)] = result[:, c * 128 : c * 128 + 128]
+            both[c, pl.ds(i * 512, 512)] = result[:, c * 128 : c * 128 + 128]
 
     result = times(patches[256], wkvx[...])
     for c in range(4):
@@ -238,9 +234,7 @@
 
     img_recv[me] = img[...]
 
-    @pl.loop(1, GROUPS)
-    def _(k):
-        p = peer(k)
+    for p in others:
         img_copy(p, p).wait_recv()
 
     to_scalars = pltpu.make_async_copy(img_recv, img_s, img_sem)
@@ -251,46 +245,56 @@
     second_mask = (1 - low.astype(f32)).astype(bf16)
     column = lax.broadcasted_iota(jnp.int32, (1, KEYS), 1)
 
-    def attend(rows, image):
-        a, b = rows[0:32], rows[32:48]
-        top = jnp.concatenate([a * first_mask, a * second_mask, jnp.zeros((32, 128), bf16)], axis=0)
-        bottom = jnp.concatenate([jnp.zeros((64, 128), bf16), b * first_mask, b * second_mask], axis=0)
-        q = jnp.concatenate([top, bottom], axis=1)
-        scores = times(q, keys[image])
-        scores = jnp.where(column < PATCH, scores * 0.125, -jnp.inf)
-        raised = jnp.exp(scores - jnp.max(scores, axis=1, keepdims=True))
-        weights = (raised / jnp.sum(raised, axis=1, keepdims=True)).astype(bf16)
-        c = jnp.dot(weights, values[image], preferred_element_type=f32)
-        c01 = jnp.where(low, c[0:32, :128], c[32:64, :128])
-        c2 = jnp.where(low, c[64:80, 128:], c[80:96, 128:])
-        return jnp.concatenate([c01, c2], axis=0).astype(bf16)
+    factor = 0.125 * 1.4426950408889634
+
+    def attend(slots, images):
+        scores, weights, context, packed = [], [], [], []
+        for slot, image in zip(slots, images):
+            rows = qrecv[slot]
+            a, b = rows[0:32], rows[32:48]
+            top = jnp.concatenate([a * first_mask, a * second_mask, jnp.zeros((32, 128), bf16)], axis=0)
+            bottom = jnp.concatenate([jnp.zeros((64, 128), bf16), b * first_mask, b * second_mask], axis=0)
+            scores.append(times(jnp.concatenate([top, bottom], axis=1), keys[image]))
+        for s in scores:
+            s = jnp.where(column < PATCH, s, -jnp.inf)
+            e = jnp.exp2((s - jnp.max(s, axis=1, keepdims=True)) * factor)
+            weights.append((e * (1.0 / jnp.sum(e, axis=1, keepdims=True))).astype(bf16))
+        for w, image in zip(weights, images):
+            context.append(jnp.dot(w, values[image], preferred_element_type=f32))
+        for c in context:
+            c01 = jnp.where(low, c[0:32, :128], c[32:64, :128])
+            c2 = jnp.where(low, c[64:80, 128:], c[80:96, 128:])
+            packed.append(jnp.concatenate([c01, c2], axis=0).astype(bf16))
+        return packed
 
     qrecv[pl.ds(me * SLOTS, SLOTS)] = qsend[pl.ds(me * SLOTS, SLOTS)]
 
-    @pl.loop(0, GROUPS)
-    def _(k):
-        p = peer(k)
-
-        @pl.when(k > 0)
-        def _():
-            q_copy(p, p).wait_recv()
-
-        done = [attend(qrecv[p * SLOTS + s], img_s[p, 0, me * SLOTS + s]) for s in range(SLOTS)]
-        for s in range(SLOTS):
-            csend[p * SLOTS + s] = done[s]
-
-        @pl.when(k > 0)
-        def _():
-            c_copy(p, me).start()
+    @pl.loop(0, GROUPS // NX)
+    def _(n):
+        four = [peer(n * NX + i) for i in range(NX)]
+        for i, p in enumerate(four):
+            if i:
+                q_copy(p, p).wait_recv()
+            else:
+                pl.when(n > 0)(q_copy(p, p).wait_recv)
+        slots = [p * SLOTS + s for p in four for s in range(SLOTS)]
+        images = [img_s[p, 0, me * SLOTS + s] for p in four for s in range(SLOTS)]
+        for slot, rows in zip(slots, attend(slots, images)):
+            csend[slot] = rows
+        for i, p in enumerate(four):
+            if i:
+                c_copy(p, me).start()
+            else:
+                pl.when(n > 0)(c_copy(p, me).start)
 
     for i in range(3):
         weights_1(i)
 
     crecv[pl.ds(me * SLOTS, SLOTS)] = csend[pl.ds(me * SLOTS, SLOTS)]
 
-    @pl.loop(1, GROUPS)
-    def _(k):
-        p = peer(k)
+    for p in others:
+        img_copy(p, p).wait_send()
+        q_copy(p, p).wait_send()
         c_copy(p, p).wait_recv()
 
     @pl.loop(0, PAIRS)
@@ -303,6 +307,9 @@
     for k in range(1, TENSOR):
         y_copy(y_peer(k), ty).start()
     yrecv[ty] = ysend[ty]
+
+    for p in others:
+        c_copy(p, p).wait_send()
 
     for i in range(3):
         weights_2(i)
@@ -327,14 +334,20 @@
         total = total + jnp.dot(rows, wout[t], preferred_element_type=f32)
     first_norm = norm(total).astype(bf16)
 
-    for i in (1, 2):
-        weights_3(i)
+    weights_3(1)
+    weights_3(2)
     total = first_norm.astype(f32)
+
+    def up(t):
+        return jnp.dot(first_norm, win[t], preferred_element_type=f32)
+
+    later = up(0)
     for t in range(TENSOR):
-        for n in range(0, D, 256):
-            up = jnp.dot(first_norm, win[t, :, n : n + 256], preferred_element_type=f32)
-            hidden = (0.5 * up * (1.0 + lax.erf(up * 0.7071067811865476))).astype(bf16)
-            total = total + jnp.dot(hidden, wdn[t, n : n + 256, :], preferred_element_type=f32)
+        now = later
+        if t < TENSOR - 1:
+            later = up(t + 1)
+        hidden = (0.5 * now * (1.0 + lax.erf(now * 0.7071067811865476))).astype(bf16)
+        total = total + jnp.dot(hidden, wdn[t], preferred_element_type=f32)
     score = jnp.sum(norm(total) * match_ref[...].astype(f32).reshape(1, D), axis=-1, keepdims=True)
     score = jnp.mean(score.reshape(8, NQ, 1), axis=1)
 
@@ -368,23 +381,15 @@
     def o_copy(dst, src):
         return remote(osend, orecv.at[src], o_ss.at[dst], o_rs.at[src], query=dst)
 
-    @pl.loop(1, GROUPS)
-    def _(k):
-        o_copy(peer(k), me).start()
-
-    @pl.loop(1, GROUPS)
-    def _(k):
-        p = peer(k)
+    for p in reversed(others):
+        o_copy(p, me).start()
+
+    for p in others:
         o_copy(p, p).wait_recv()
 
     out_ref[...] = orecv[...].reshape(GROUPS, 128)[:, :PAIRS]
 
-    @pl.loop(1, GROUPS)
-    def _(k):
-        p = peer(k)
-        img_copy(p, p).wait_send()
-        q_copy(p, p).wait_send()
-        c_copy(p, p).wait_send()
+    for p in others:
         o_copy(p, p).wait_send()
 
     for k in range(1, TENSOR):

time: 97.4 us -> 78.9 us (0.81)
  Pallas kernels: 95.9 us -> 77.4 us
    pallas_call x1, Pallas kernels: 95.9 us -> 77.4 us  [body(): pl.pallas_call(kernel, out_shape=jax.ShapeDtypeStruct((GROUPS, PAIRS), f3...]
where the time goes in v3:
time: 78.9 us; the launch traced here: 78.7 us
  Pallas kernels  77.4 us (98%)
  local copies, waits for them, and re-layouts  1.32 us (2%)
    pallas_call x1, Pallas kernels, body(): pl.pallas_call(kernel, out_shape=jax.ShapeDtypeStruct((GROUPS, PAIRS), f3...  77.4 us

profile of v3, /device:TPU:1, one launch (start us, length us, event | category | flops | bytes accessed | tf_op | source)
XLA Modules:
  0.0 78.7 jit_solution(15880681880290970149)
XLA Ops:
  0.0 77.4 %shard_map.109 = f32[32,32]{1,0:T(8,128)} custom-call(s32[1,32]{1,0:T(1,128)} %bitcast.12, s32[1,32]{1,0:T(1,128)} %bitcast.13, bf16[768]{0:T(1024)(128)(2,1)} %match_ref.1, bf16[32,32,768]{2,1,0:T(8,128)(2,1)} %states_h.1, bf16[257,8,1408]{2,1,0:T(8,128)(2,1)} %bitcast.8, bf16[192,768]{1,0:T(8,128)(2,1)} %bitcast.11, bf16[192,1408]{1,0:T(8,128)(2,1)} %bitcast.9, ...), custom_call_target="tpu_custom_call" | custom-call | tf_op jit(solution)/shard_map/pallas_call | solution.py:415
  77.4 1.3 %copy.13 = f32[32,32]{1,0:T(8,128)} copy(f32[32,32]{1,0:T(8,128)} %shard_map.109) | data formatting | bytes 8192

commit v4 on v3

--- a/solution.py
+++ b/solution.py
@@ -30,9 +30,9 @@
     out_ref,
     states, patches, wqx, wkvx, both, img, idx_v, idx,
     qpk, qsend, qrecv, csend, crecv, keys, values, img_recv, img_s,
-    ysend, yrecv, wout, win, wdn, fsend, frecv, ssend, srecv, osend, orecv,
+    ysend, yrecv, wout, win, wdn, fsend, frecv, osend, orecv,
     load_sem, img_ss, img_rs, q_ss, q_rs, c_ss, c_rs, y_ss, y_rs,
-    w_own, w_ss, w_rs, f_ss, f_rs, s_ss, s_rs, o_ss, o_rs, img_sem, idx_sem,
+    w_own, w_ss, w_rs, f_ss, f_rs, o_ss, o_rs, img_sem, idx_sem,
 ):
     me = lax.axis_index("query")
     core = lax.axis_index("owner")
@@ -81,7 +81,8 @@
 
     for k in range(1, TENSOR):
         pl.semaphore_signal(barrier, inc=1, device_id={"tensor": y_peer(k)}, device_id_type=MESH)
-    pl.semaphore_signal(barrier, inc=1, device_id={"owner": 1 - core}, device_id_type=MESH)
+    for k in range(TENSOR):
+        pl.semaphore_signal(barrier, inc=1, device_id={"owner": 1 - core, "tensor": y_peer(k)}, device_id_type=MESH)
 
     wide = (PAIRS, 128)
     lanes = lax.broadcasted_iota(jnp.int32, wide, 1)
@@ -116,29 +117,8 @@
     last = jnp.where(low[None], q[:, :16, 128:], q[:, 16:, 128:])
     qpk[...] = jnp.concatenate([q[:, :, :128], last], axis=1).astype(bf16)
 
-    pl.semaphore_wait(barrier, GROUPS + TENSOR - 1)
+    pl.semaphore_wait(barrier, GROUPS - 1 + 2 * TENSOR - 1)
     to_index.wait()
-
-    def img_copy(dst, src):
-        return remote(img, img_recv.at[src], img_ss.at[dst], img_rs.at[src], query=dst)
-
-    for p in others:
-        img_copy(p, me).start()
-
-    def of(ref, p):
-        return ref.at[pl.ds(p * SLOTS, SLOTS)]
-
-    def q_copy(dst, src):
-        return remote(of(qsend, dst), of(qrecv, src), q_ss.at[dst], q_rs.at[src], query=dst)
-
-    def c_copy(dst, src):
-        return remote(of(csend, dst), of(crecv, src), c_ss.at[dst], c_rs.at[src], query=dst)
-
-    for k, p in enumerate(peers):
-        for s in range(SLOTS):
-            qsend[p * SLOTS + s] = qpk[idx[0, p * SLOTS + s]]
-        if k:
-            q_copy(p, me).start()
 
     right, left, across = y_peer(1), y_peer(3), y_peer(2)
     shards = ((wout_h, wout, 192), (win_h, win, D), (wdn_h, wdn, D))
@@ -205,6 +185,27 @@
 
     for i in range(3):
         weights_0(i)
+
+    def img_copy(dst, src):
+        return remote(img, img_recv.at[src], img_ss.at[dst], img_rs.at[src], query=dst)
+
+    for p in others:
+        img_copy(p, me).start()
+
+    def of(ref, p):
+        return ref.at[pl.ds(p * SLOTS, SLOTS)]
+
+    def q_copy(dst, src):
+        return remote(of(qsend, dst), of(qrecv, src), q_ss.at[dst], q_rs.at[src], query=dst)
+
+    def c_copy(dst, src):
+        return remote(of(csend, dst), of(crecv, src), c_ss.at[dst], c_rs.at[src], query=dst)
+
+    for k, p in enumerate(peers):
+        for s in range(SLOTS):
+            qsend[p * SLOTS + s] = qpk[idx[0, p * SLOTS + s]]
+        if k:
+            q_copy(p, me).start()
 
     for copy in loads[2:]:
         copy.wait()
@@ -277,6 +278,11 @@
                 q_copy(p, p).wait_recv()
             else:
                 pl.when(n > 0)(q_copy(p, p).wait_recv)
+        @pl.when(n == GROUPS // NX - 1)
+        def _():
+            for i in range(3):
+                weights_1(i)
+
         slots = [p * SLOTS + s for p in four for s in range(SLOTS)]
         images = [img_s[p, 0, me * SLOTS + s] for p in four for s in range(SLOTS)]
         for slot, rows in zip(slots, attend(slots, images)):
@@ -287,9 +293,6 @@
             else:
                 pl.when(n > 0)(c_copy(p, me).start)
 
-    for i in range(3):
-        weights_1(i)
-
     crecv[pl.ds(me * SLOTS, SLOTS)] = csend[pl.ds(me * SLOTS, SLOTS)]
 
     for p in others:
@@ -355,22 +358,19 @@
     pair = lax.broadcasted_iota(jnp.int32, (8, 128), 0) + (core * PAIRS + ty * 8)
     row = jnp.sum(jnp.where(lane == pair, score, 0.0), axis=0, keepdims=True)
     fsend[...] = row
-
-    def f_copy(dst, src):
-        return remote(fsend, frecv.at[src], f_ss.at[dst], f_rs.at[src], tensor=dst)
-
-    for k in range(1, TENSOR):
-        f_copy(y_peer(k), ty).start()
-    frecv[ty] = row
-    for k in range(1, TENSOR):
-        t = y_peer(k)
-        f_copy(t, t).wait_recv()
-    row = frecv[0] + frecv[1] + frecv[2] + frecv[3]
-    ssend[...] = row
-    s_copy = remote(ssend, srecv, s_ss, s_rs, owner=1 - core)
-    s_copy.start()
-    s_copy.wait_recv()
-    row = row + srecv[...]
+    frecv[core, ty] = row
+    group = [(c, k) for c in (0, 1) for k in range(TENSOR) if c or k]
+
+    def f_copy(c, k, receive=False):
+        device = {"owner": lax.rem(core + c, 2), "tensor": y_peer(k)}
+        at = (device["owner"], device["tensor"]) if receive else (core, ty)
+        return remote(fsend, frecv.at[at], f_ss.at[c, k], f_rs.at[at], **device)
+
+    for c, k in reversed(group):
+        f_copy(c, k).start()
+    for c, k in group:
+        f_copy(c, k, True).wait_recv()
+    row = jnp.sum(frecv[...].reshape(2 * TENSOR, 128), axis=0, keepdims=True)
     valid = lax.broadcasted_iota(jnp.int32, (1, 128), 1) < 2 * PAIRS
     partition = jnp.sum(jnp.where(valid, jnp.exp(row), 0.0), axis=1, keepdims=True)
     row = row - jnp.log(partition)
@@ -395,8 +395,8 @@
     for k in range(1, TENSOR):
         t = y_peer(k)
         y_copy(t, t).wait_send()
-        f_copy(t, t).wait_send()
-    s_copy.wait_send()
+    for c, k in group:
+        f_copy(c, k).wait_send()
     for i in range(3):
         first_hop(i, True).wait_send()
         first_hop(i, False).wait_send()
@@ -441,9 +441,7 @@
             pltpu.VMEM((TENSOR, D, D), bf16),
             pltpu.VMEM((TENSOR, D, D), bf16),
             pltpu.VMEM((1, 128), f32),
-            pltpu.VMEM((TENSOR, 1, 128), f32),
-            pltpu.VMEM((1, 128), f32),
-            pltpu.VMEM((1, 128), f32),
+            pltpu.VMEM((2, TENSOR, 1, 128), f32),
             pltpu.VMEM((1, 128), f32),
             pltpu.VMEM((GROUPS, 1, 128), f32),
             dma((5,)),
@@ -452,8 +450,7 @@
             dma((GROUPS,)), dma((GROUPS,)),
             dma((TENSOR,)), dma((TENSOR,)),
             dma((3,)), dma((3, 8)), dma((3, 8)),
-            dma((TENSOR,)), dma((TENSOR,)),
-            dma, dma,
+            dma((2, TENSOR)), dma((2, TENSOR)),
             dma((GROUPS,)), dma((GROUPS,)),
             dma, dma,
         ],

time: 78.9 us -> 77.5 us (0.982)
  Pallas kernels: 77.4 us -> 76 us
    pallas_call x1, Pallas kernels: 77.4 us -> 76 us  [body(): pl.pallas_call(kernel, out_shape=jax.ShapeDtypeStruct((GROUPS, PAIRS), f3...]
where the time goes in v4:
time: 77.5 us; the launch traced here: 77.3 us
  Pallas kernels  76 us (98%)
  local copies, waits for them, and re-layouts  1.32 us (2%)
    pallas_call x1, Pallas kernels, body(): pl.pallas_call(kernel, out_shape=jax.ShapeDtypeStruct((GROUPS, PAIRS), f3...  76 us

profile of v4, /device:TPU:1, one launch (start us, length us, event | category | flops | bytes accessed | tf_op | source)
XLA Modules:
  0.0 77.3 jit_solution(1002496151682582976)
XLA Ops:
  0.0 76.0 %shard_map.109 = f32[32,32]{1,0:T(8,128)} custom-call(s32[1,32]{1,0:T(1,128)} %bitcast.12, s32[1,32]{1,0:T(1,128)} %bitcast.13, bf16[768]{0:T(1024)(128)(2,1)} %match_ref.1, bf16[32,32,768]{2,1,0:T(8,128)(2,1)} %states_h.1, bf16[257,8,1408]{2,1,0:T(8,128)(2,1)} %bitcast.8, bf16[192,768]{1,0:T(8,128)(2,1)} %bitcast.11, bf16[192,1408]{1,0:T(8,128)(2,1)} %bitcast.9, ...), custom_call_target="tpu_custom_call" | custom-call | tf_op jit(solution)/shard_map/pallas_call | solution.py:415
  76.0 1.3 %copy.13 = f32[32,32]{1,0:T(8,128)} copy(f32[32,32]{1,0:T(8,128)} %shard_map.109) | data formatting | bytes 8192

commit v5 on v4

--- a/solution.py
+++ b/solution.py
@@ -71,7 +71,7 @@
             )
         )
     ]
-    for copy in loads:
+    for copy in loads[:2]:
         copy.start()
 
     barrier = pltpu.get_barrier_semaphore()
@@ -107,6 +107,8 @@
 
     loads[0].wait()
     loads[1].wait()
+    for copy in loads[2:]:
+        copy.start()
     wqx[192:256] = wqx[128:192]
     low = lax.broadcasted_iota(jnp.int32, (1, 128), 1) < 64
 
@@ -278,9 +280,10 @@
                 q_copy(p, p).wait_recv()
             else:
                 pl.when(n > 0)(q_copy(p, p).wait_recv)
-        @pl.when(n == GROUPS // NX - 1)
-        def _():
-            for i in range(3):
+        for i in range(3):
+
+            @pl.when(n == GROUPS // NX - 3 + i)
+            def _():
                 weights_1(i)
 
         slots = [p * SLOTS + s for p in four for s in range(SLOTS)]
@@ -300,16 +303,16 @@
         q_copy(p, p).wait_send()
         c_copy(p, p).wait_recv()
 
-    @pl.loop(0, PAIRS)
-    def _(j):
-        ysend[j // 8, j % 8] = crecv[idx[1, j]]
-
     def y_copy(dst, src):
         return remote(ysend.at[dst], yrecv.at[src], y_ss.at[dst], y_rs.at[src], tensor=dst)
 
-    for k in range(1, TENSOR):
-        y_copy(y_peer(k), ty).start()
-    yrecv[ty] = ysend[ty]
+    for k in (2, 1, 3):
+        t = y_peer(k)
+        for j in range(8):
+            ysend[t, j] = crecv[idx[1, t * 8 + j]]
+        y_copy(t, ty).start()
+    for j in range(8):
+        yrecv[ty, j] = crecv[idx[1, ty * 8 + j]]
 
     for p in others:
         c_copy(p, p).wait_send()
@@ -319,17 +322,16 @@
     weights_3(0)
     for t in range(TENSOR):
         wout[t, 192:256] = wout[t, 128:192]
-    for k in range(1, TENSOR):
-        t = y_peer(k)
-        y_copy(t, t).wait_recv()
-
     def norm(v):
         mean = jnp.mean(v, axis=-1, keepdims=True)
         squares = jnp.mean(v * v, axis=-1, keepdims=True)
         return (v - mean) * lax.rsqrt(squares - mean * mean + EPSILON)
 
     total = states[pl.ds(ty * 8, 8)].reshape(ROWS, D).astype(f32)
-    for t in range(TENSOR):
+    for k in (0, 1, 3, 2):
+        t = y_peer(k)
+        if k:
+            y_copy(t, t).wait_recv()
         c = yrecv[t]
         b = c[:, 32:]
         second = jnp.concatenate([b * first_mask[None], b * second_mask[None]], axis=1)
@@ -383,14 +385,6 @@
 
     for p in reversed(others):
         o_copy(p, me).start()
-
-    for p in others:
-        o_copy(p, p).wait_recv()
-
-    out_ref[...] = orecv[...].reshape(GROUPS, 128)[:, :PAIRS]
-
-    for p in others:
-        o_copy(p, p).wait_send()
 
     for k in range(1, TENSOR):
         t = y_peer(k)
@@ -404,6 +398,13 @@
         second_hop(i, False).wait_send()
         for which in range(4):
             sibling(i, which).wait_send()
+    for p in others:
+        o_copy(p, p).wait_send()
+
+    for p in others:
+        o_copy(p, p).wait_recv()
+
+    out_ref[...] = orecv[...].reshape(GROUPS, 128)[:, :PAIRS]
 
 
 def body(

time: 77.5 us -> 77.2 us (level)
  no operation moved by 1% of the time
where the time goes in v5:
time: 77.2 us; the launch traced here: 77 us
  Pallas kernels  75.7 us (98%)
  local copies, waits for them, and re-layouts  1.32 us (2%)
    pallas_call x1, Pallas kernels, body(): pl.pallas_call(kernel, out_shape=jax.ShapeDtypeStruct((GROUPS, PAIRS), f3...  75.7 us

profile of v5, /device:TPU:1, one launch (start us, length us, event | category | flops | bytes accessed | tf_op | source)
XLA Modules:
  0.0 77.0 jit_solution(14343331374477468637)
XLA Ops:
  0.0 75.7 %shard_map.109 = f32[32,32]{1,0:T(8,128)} custom-call(s32[1,32]{1,0:T(1,128)} %bitcast.12, s32[1,32]{1,0:T(1,128)} %bitcast.13, bf16[768]{0:T(1024)(128)(2,1)} %match_ref.1, bf16[32,32,768]{2,1,0:T(8,128)(2,1)} %states_h.1, bf16[257,8,1408]{2,1,0:T(8,128)(2,1)} %bitcast.8, bf16[192,768]{1,0:T(8,128)(2,1)} %bitcast.11, bf16[192,1408]{1,0:T(8,128)(2,1)} %bitcast.9, ...), custom_call_target="tpu_custom_call" | custom-call | tf_op jit(solution)/shard_map/pallas_call | solution.py:416
  75.7 1.3 %copy.13 = f32[32,32]{1,0:T(8,128)} copy(f32[32,32]{1,0:T(8,128)} %shard_map.109) | data formatting | bytes 8192

commit v6 on v5

--- a/solution.py
+++ b/solution.py
@@ -26,12 +26,12 @@
 
 
 def kernel(
-    source, image, match_ref, states_h, patches_h, wq_h, wk_h, wv_h, wout_h, win_h, wdn_h,
+    source_h, image_h, match_h, states_h, patches_h, wq_h, wk_h, wv_h, wout_h, win_h, wdn_h,
     out_ref,
-    states, patches, wqx, wkvx, both, img, idx_v, idx,
+    source, image, match_ref, states, patches, wqx, wkvx, both, img, idx_v, idx,
     qpk, qsend, qrecv, csend, crecv, keys, values, img_recv, img_s,
     ysend, yrecv, wout, win, wdn, fsend, frecv, osend, orecv,
-    load_sem, img_ss, img_rs, q_ss, q_rs, c_ss, c_rs, y_ss, y_rs,
+    small_sem, load_sem, img_ss, img_rs, q_ss, q_rs, c_ss, c_rs, y_ss, y_rs,
     w_own, w_ss, w_rs, f_ss, f_rs, o_ss, o_rs, img_sem, idx_sem,
 ):
     me = lax.axis_index("query")
@@ -71,7 +71,11 @@
             )
         )
     ]
-    for copy in loads[:2]:
+    small = [
+        pltpu.make_async_copy(src, dst, small_sem.at[i])
+        for i, (src, dst) in enumerate(((source_h, source), (image_h, image), (match_h, match_ref)))
+    ]
+    for copy in small + loads[:2]:
         copy.start()
 
     barrier = pltpu.get_barrier_semaphore()
@@ -94,6 +98,8 @@
     def column_of(v):
         return jnp.sum(jnp.where(lanes == number, v, 0), axis=1, keepdims=True)
 
+    for copy in small:
+        copy.wait()
     source_row = jnp.concatenate([source[...], jnp.full((1, 128 - PAIRS), -1, jnp.int32)], axis=1)
     image_row = jnp.concatenate([image[...], jnp.zeros((1, 128 - PAIRS), jnp.int32)], axis=1)
     earlier = (column_of(source_row) == source_row) & (number < lanes)
@@ -416,9 +422,12 @@
     return pl.pallas_call(
         kernel,
         out_shape=jax.ShapeDtypeStruct((GROUPS, PAIRS), f32),
-        in_specs=[vmem] * 3 + [hbm] * 8,
+        in_specs=[hbm] * 11,
         out_specs=vmem,
         scratch_shapes=[
+            pltpu.VMEM((1, PAIRS), jnp.int32),
+            pltpu.VMEM((1, PAIRS), jnp.int32),
+            pltpu.VMEM((D,), bf16),
             pltpu.VMEM((PAIRS, NQ, D), bf16),
             pltpu.VMEM((PATCH, IMAGES, VIS), bf16),
             pltpu.VMEM((256, D), bf16),
@@ -445,7 +454,7 @@
             pltpu.VMEM((2, TENSOR, 1, 128), f32),
             pltpu.VMEM((1, 128), f32),
             pltpu.VMEM((GROUPS, 1, 128), f32),
-            dma((5,)),
+            dma((3,)), dma((5,)),
             dma((GROUPS,)), dma((GROUPS,)),
             dma((GROUPS,)), dma((GROUPS,)),
             dma((GROUPS,)), dma((GROUPS,)),

time: 77.2 us -> 76.6 us (level)
  no operation moved by 1% of the time
where the time goes in v6:
time: 76.6 us; the launch traced here: 76.4 us
  Pallas kernels  75.1 us (98%)
  local copies, waits for them, and re-layouts  1.32 us (2%)
    pallas_call x1, Pallas kernels, body(): pl.pallas_call(kernel, out_shape=jax.ShapeDtypeStruct((GROUPS, PAIRS), f3...  75.1 us

profile of v6, /device:TPU:1, one launch (start us, length us, event | category | flops | bytes accessed | tf_op | source)
XLA Modules:
  0.0 76.4 jit_solution(4391938283683909435)
XLA Ops:
  0.0 75.1 %shard_map.109 = f32[32,32]{1,0:T(8,128)} custom-call(s32[1,32]{1,0:T(1,128)} %bitcast.12, s32[1,32]{1,0:T(1,128)} %bitcast.13, bf16[768]{0:T(1024)(128)(2,1)} %match_h.1, bf16[32,32,768]{2,1,0:T(8,128)(2,1)} %states_h.1, bf16[257,8,1408]{2,1,0:T(8,128)(2,1)} %bitcast.8, bf16[192,768]{1,0:T(8,128)(2,1)} %bitcast.11, bf16[192,1408]{1,0:T(8,128)(2,1)} %bitcast.9, ...), custom_call_target="tpu_custom_call" | custom-call | tf_op jit(solution)/shard_map/pallas_call | solution.py:422
  75.1 1.3 %copy.13 = f32[32,32]{1,0:T(8,128)} copy(f32[32,32]{1,0:T(8,128)} %shard_map.109) | data formatting | bytes 8192

commit v7 on v6

--- a/solution.py
+++ b/solution.py
@@ -432,7 +432,7 @@
             pltpu.VMEM((PATCH, IMAGES, VIS), bf16),
             pltpu.VMEM((256, D), bf16),
             pltpu.VMEM((512, VIS), bf16),
-            pltpu.VMEM((4, PATCH * IMAGES, 128), f32),
+            pltpu.VMEM((4, (PATCH + 7) * IMAGES, 128), f32),
             pltpu.VMEM((1, 128), jnp.int32),
             pltpu.VMEM((2, 128), jnp.int32),
             pltpu.SMEM((2, 128), jnp.int32),

time: 76.6 us -> 76.6 us (level)
  no operation moved by 1% of the time
where the time goes in v7:
time: 76.6 us; the launch traced here: 76.4 us
  Pallas kernels  75.1 us (98%)
  local copies, waits for them, and re-layouts  1.32 us (2%)
    pallas_call x1, Pallas kernels, body(): pl.pallas_call(kernel, out_shape=jax.ShapeDtypeStruct((GROUPS, PAIRS), f3...  75.1 us

profile of v7, /device:TPU:1, one launch (start us, length us, event | category | flops | bytes accessed | tf_op | source)
XLA Modules:
  0.0 76.4 jit_solution(7169783479011703649)
XLA Ops:
  0.0 75.1 %shard_map.109 = f32[32,32]{1,0:T(8,128)} custom-call(s32[1,32]{1,0:T(1,128)} %bitcast.12, s32[1,32]{1,0:T(1,128)} %bitcast.13, bf16[768]{0:T(1024)(128)(2,1)} %match_h.1, bf16[32,32,768]{2,1,0:T(8,128)(2,1)} %states_h.1, bf16[257,8,1408]{2,1,0:T(8,128)(2,1)} %bitcast.8, bf16[192,768]{1,0:T(8,128)(2,1)} %bitcast.11, bf16[192,1408]{1,0:T(8,128)(2,1)} %bitcast.9, ...), custom_call_target="tpu_custom_call" | custom-call | tf_op jit(solution)/shard_map/pallas_call | solution.py:422
  75.1 1.3 %copy.13 = f32[32,32]{1,0:T(8,128)} copy(f32[32,32]{1,0:T(8,128)} %shard_map.109) | data formatting | bytes 8192
